TPU v7x, 1024 devices: a whole 4x4x32 slice. The times are simulated.
1024 devices in a mesh: dp: 32 (over x, y, core), fsdp: 32 (over z).
Axes of the slice: x: 4, y: 4, z: 32, core: 2. Of those that a mesh axis runs over, the one named last changes fastest.
Arguments:
- events: bfloat16 [3072, 128, 1024], P(('dp', 'fsdp')), may hold values from -6 to 6
- query_weight: bfloat16 [1024, 512], P('fsdp'), may hold values from -0.1875 to 0.1875
- keys: bfloat16 [3072, 128, 512], P(('dp', 'fsdp')), may hold values from -6 to 6
- values: bfloat16 [3072, 128, 512], P(('dp', 'fsdp')), may hold values from -48 to 48
- gates: bfloat16 [3072, 128, 512], P(('dp', 'fsdp')), may hold values from -6 to 6
- cotangent: bfloat16 [3072, 128, 512], P(('dp', 'fsdp')), may hold values from -6 to 6
- lengths: int32 [3072], replicated, may hold values from 1 to 128, as said below
Outputs:
- grad_keys: bfloat16 [3072, 128, 512], P(('dp', 'fsdp'))
- grad_values: bfloat16 [3072, 128, 512], P(('dp', 'fsdp'))
- grad_gates: bfloat16 [3072, 128, 512], P(('dp', 'fsdp'))
- grad_weight: float32 [1024, 512], P('fsdp')
Inputs may be any that keep to these rules, and one draw needn't show every extreme that they name: Each sequence fills the first lengths[b] events of its slot of 128 events; the rest is padding that no output reads.
All inputs are finite; a program needn't handle non-finite values.
Results may differ from a plain program's by a relative error of at most 0.015.
Values may be sent and summed in bfloat16 or wider, within the bound.
A program may use at most 32 MiB of HBM per device.

v0:
```python
import math

import jax
import jax.numpy as jnp
from jax import lax
from jax.sharding import PartitionSpec as P

HEADS = 4
BLK = 64


EPSILON = 1e-06


def slot_grads(queries, key_rows, value_rows, gate_rows, upstream_rows, length, head_count):
    row_count = queries.shape[0]
    head_width = queries.shape[1]
    head_depth = head_width // head_count
    score_scale = 1.0 / math.sqrt(head_depth)
    query_h = queries.reshape(row_count, head_count, head_depth)
    keys_h = key_rows.reshape(row_count, head_count, head_depth)
    values_h = value_rows.reshape(row_count, head_count, head_depth)
    scores = (
        jnp.einsum("qhd,khd->hqk", query_h, keys_h, preferred_element_type=jnp.float32)
        * score_scale
    )
    places = lax.iota(jnp.int32, row_count)
    causal = (places[None, :] <= places[:, None]) & (places[:, None] < length)
    weight_mask = causal.astype(jnp.float32)[None]
    inverse = 1.0 / length.astype(jnp.float32)
    sigmoid = jax.nn.sigmoid(scores)
    attention = (scores * sigmoid * weight_mask * inverse).astype(jnp.bfloat16)
    mixed_rows = jnp.einsum(
        "hqk,khd->qhd", attention, values_h, preferred_element_type=jnp.float32
    ).reshape(row_count, head_width)
    centred = mixed_rows - jnp.mean(mixed_rows, axis=1, keepdims=True)
    inv_std = lax.rsqrt(jnp.mean(centred * centred, axis=1, keepdims=True) + EPSILON)
    normed = centred * inv_std
    upstream = upstream_rows.astype(jnp.float32)
    grad_gates = (upstream * normed).astype(jnp.bfloat16)
    valid_rows = (places < length).astype(jnp.float32)[:, None]
    grad_normed = upstream * gate_rows.astype(jnp.float32) * valid_rows
    grad_mixed = inv_std * (
        grad_normed
        - jnp.mean(grad_normed, axis=1, keepdims=True)
        - normed * jnp.mean(grad_normed * normed, axis=1, keepdims=True)
    )
    grad_mixed = grad_mixed.astype(jnp.bfloat16).reshape(row_count, head_count, head_depth)
    grad_values = jnp.einsum(
        "hqk,qhd->khd", attention, grad_mixed, preferred_element_type=jnp.float32
    )
    grad_attention = jnp.einsum(
        "qhd,khd->hqk", grad_mixed, values_h, preferred_element_type=jnp.float32
    )
    grad_scores = (
        grad_attention * sigmoid * (1.0 + scores * (1.0 - sigmoid)) * weight_mask * inverse
    ).astype(jnp.bfloat16)
    grad_query = (
        jnp.einsum("hqk,khd->qhd", grad_scores, keys_h, preferred_element_type=jnp.float32)
        * score_scale
    )
    grad_keys = (
        jnp.einsum("hqk,qhd->khd", grad_scores, query_h, preferred_element_type=jnp.float32)
        * score_scale
    )
    return (
        grad_query.reshape(row_count, head_width).astype(jnp.bfloat16),
        grad_keys.reshape(row_count, head_width).astype(jnp.bfloat16),
        grad_values.reshape(row_count, head_width).astype(jnp.bfloat16),
        grad_gates,
    )


def prefix_branch(row_count, slot_span):

    def run_prefix(operands):
        queries, key_rows, value_rows, gate_rows, upstream_rows, length = operands
        if row_count == 0:
            empty = jnp.zeros((slot_span, queries.shape[1]), jnp.bfloat16)
            return (empty, empty, empty, empty)
        results = slot_grads(
            queries[:row_count],
            key_rows[:row_count],
            value_rows[:row_count],
            gate_rows[:row_count],
            upstream_rows[:row_count],
            length,
            HEADS,
        )
        return tuple((jnp.pad(result, ((0, slot_span - row_count), (0, 0))) for result in results))

    return run_prefix


def attend(operands):
    slot_span = operands[0].shape[0]
    block_count = slot_span // BLK
    live_blocks = jnp.minimum((operands[5] + BLK - 1) // BLK, block_count)
    branches = [prefix_branch(blocks * BLK, slot_span) for blocks in range(block_count + 1)]
    return lax.switch(live_blocks, branches, operands)


def shards(events, query_weight, keys, values, gates, cotangent, lengths):
    slot_count, slot_span, model_width = events.shape
    head_width = query_weight.shape[1]
    flat_events = events.reshape(slot_count * slot_span, model_width)
    columns = flat_events
    queries = jnp.dot(
        columns,
        lax.all_gather(query_weight, "fsdp", axis=0, tiled=True),
        preferred_element_type=jnp.float32,
    )
    queries = queries.astype(jnp.bfloat16).reshape(slot_count, slot_span, head_width)
    dp_count = lax.axis_size("dp")
    fsdp_count = lax.axis_size("fsdp")
    dp_place = lax.axis_index("dp")
    fsdp_place = lax.axis_index("fsdp")
    device_row = dp_place * fsdp_count + fsdp_place
    own_lengths = lax.dynamic_slice_in_dim(lengths, device_row * slot_count, slot_count)
    operands = (queries, keys, values, gates, cotangent)
    merged = lax.map(attend, operands + (own_lengths,))
    grad_query, grad_keys, grad_values, grad_gates = merged
    grad_flat = grad_query.reshape(slot_count * slot_span, head_width)
    total_seqs = slot_count * dp_count * fsdp_count
    contract = (((0,), (0,)), ((), ()))
    columns = flat_events
    shard_rows = lax.psum_scatter(
        lax.dot_general(columns, grad_flat, contract, preferred_element_type=jnp.float32),
        "fsdp",
        scatter_dimension=0,
        tiled=True,
    )
    summed = lax.psum(shard_rows, "dp")
    return (grad_keys, grad_values, grad_gates, summed / total_seqs)


def solution(mesh):
    in_specs = (
        P(("dp", "fsdp"), None, None),
        P("fsdp", None),
        P(("dp", "fsdp"), None, None),
        P(("dp", "fsdp"), None, None),
        P(("dp", "fsdp"), None, None),
        P(("dp", "fsdp"), None, None),
        P(),
    )
    out_specs = (
        P(("dp", "fsdp"), None, None),
        P(("dp", "fsdp"), None, None),
        P(("dp", "fsdp"), None, None),
        P("fsdp", None),
    )
    return jax.shard_map(shards, mesh=mesh, in_specs=in_specs, out_specs=out_specs, check_vma=False)
```

profile of v0, /device:TPU:1, one launch (start us, length us, event | category | flops | bytes accessed | tf_op | source)
XLA Modules:
  0.0 503.7 jit_solution(12407402925880801280)
XLA Ops:
  8.0 0.8 dynamic_slice.65
  8.8 126.0 %all-gather.2.cloned.1.call-done = bf16[1024,512]{1,0:T(8,128)(2,1)} async-done(((bf16[32,512]{1,0:T(8,128)(2,1)}), bf16[1024,512]{1,0:T(8,128)(2,1)}) %all-gather.2.cloned.1.call-update) | async-done | bytes 1048592 | tf_op jit(solution)/shard_map/all_gather | solution.py:110
  134.8 1.8 convolution_convert_fusion.2
  136.6 23.8 %while.21 = (s32[]{:T(128)}, bf16[3,128,512]{2,1,0:T(8,128)(2,1)}, bf16[3,128,512]{2,1,0:T(8,128)(2,1)}, bf16[3,128,512]{2,1,0:T(8,128)(2,1)}, bf16[3,128,512]{2...) while((s32[]{:T(128)}, bf16[3,128,512]{2,1,0:T(8,128)(2,1)}, ...), condition=%wide.region_12.13_spmd, body=%wide.region_0.12_spmd.sunk | while | flops 103989648 | bytes 11088631 | solution.py:121
  137.9 5.2 %conditional.2 = (bf16[1,128,512]{2,1,0:T(8,128)(2,1)S(1)}, bf16[1,128,512]{2,1,0:T(8,128)(2,1)S(1)}, bf16[1,128,512]{2,1,0:T(8,128)(2,1)S(1)}, bf16[1,128,512]{2,1,0:T(8,128)(2,1)S(1)}) conditional(s32[]{:T(128)} %clamp.11, () %tuple.102, (bf16[3,128,512]{2,1,0:T(8,128)(2,1)S(1)}, ...), branch_computations={%region_1.1_spmd, %region_2.6_spmd.clone.clone, %region_7.11_spmd.... | conditional | flops 103989632 | bytes 10038608 | solution.py:100
  140.1 1.1 fusion.14
  141.2 1.0 fusion.10
  143.9 0.7 constant_dynamic-update-slice_fusion.7
  145.8 5.2 %conditional.2 = (bf16[1,128,512]{2,1,0:T(8,128)(2,1)S(1)}, bf16[1,128,512]{2,1,0:T(8,128)(2,1)S(1)}, bf16[1,128,512]{2,1,0:T(8,128)(2,1)S(1)}, bf16[1,128,512]{2,1,0:T(8,128)(2,1)S(1)}) conditional(s32[]{:T(128)} %clamp.11, () %tuple.102, (bf16[3,128,512]{2,1,0:T(8,128)(2,1)S(1)}, ...), branch_computations={%region_1.1_spmd, %region_2.6_spmd.clone.clone, %region_7.11_spmd.... | conditional | flops 103989632 | bytes 10038608 | solution.py:100
  148.0 1.1 fusion.14
  149.2 1.0 fusion.10
  151.1 0.7 constant_dynamic-update-slice_fusion.6
  151.8 0.7 constant_dynamic-update-slice_fusion.7
  153.8 5.2 %conditional.2 = (bf16[1,128,512]{2,1,0:T(8,128)(2,1)S(1)}, bf16[1,128,512]{2,1,0:T(8,128)(2,1)S(1)}, bf16[1,128,512]{2,1,0:T(8,128)(2,1)S(1)}, bf16[1,128,512]{2,1,0:T(8,128)(2,1)S(1)}) conditional(s32[]{:T(128)} %clamp.11, () %tuple.102, (bf16[3,128,512]{2,1,0:T(8,128)(2,1)S(1)}, ...), branch_computations={%region_1.1_spmd, %region_2.6_spmd.clone.clone, %region_7.11_spmd.... | conditional | flops 103989632 | bytes 10038608 | solution.py:100
  156.0 1.1 fusion.14
  157.1 1.0 fusion.10
  159.7 0.7 constant_dynamic-update-slice_fusion.7
  160.4 1.7 convolution_bitcast_fusion
  162.1 1.9 copy.99
  164.1 137.0 %reduce-scatter.4.cloned.1.call-done = f32[32,512]{1,0:T(8,128)} async-done(((f32[1024,512]{1,0:T(8,128)}), f32[32,512]{1,0:T(8,128)}) %reduce-scatter.4.cloned.1.call-update) | async-done | bytes 65552
  301.1 1.7 copy.100
  302.8 192.6 %all-reduce.6.cloned.1.call-done = f32[32,512]{0,1:T(8,128)} async-done(((f32[32,512]{0,1:T(8,128)}), f32[32,512]{0,1:T(8,128)}) %all-reduce.6.cloned.1.call-update) | async-done | bytes 65552 | tf_op jit(solution)/shard_map/psum | solution.py:133
  495.4 1.0 broadcast_multiply_fusion.6
  496.4 0.7 copy.90
  (96 shorter events, 10.9 us)
Async XLA Ops:
  7.2 127.7 %copy-start = (bf16[3,128,1024]{2,1,0:T(8,128)(2,1)S(1)}, bf16[3,128,1024]{2,1,0:T(8,128)(2,1)}, u32[]{:S(2)}) copy-start(bf16[3,128,1024]{2,1,0:T(8,128)(2,1)} %param.12) | copy-start | bytes 2359300
  7.2 129.4 %copy-start.2 = (bf16[3,128,512]{2,1,0:T(8,128)(2,1)S(1)}, bf16[3,128,512]{2,1,0:T(8,128)(2,1)}, u32[]{:S(2)}) copy-start(bf16[3,128,512]{2,1,0:T(8,128)(2,1)} %param.15) | copy-start | bytes 1179652
  7.2 129.4 %copy-start.1 = (bf16[3,128,512]{2,1,0:T(8,128)(2,1)S(1)}, bf16[3,128,512]{2,1,0:T(8,128)(2,1)}, u32[]{:S(2)}) copy-start(bf16[3,128,512]{2,1,0:T(8,128)(2,1)} %param.14) | copy-start | bytes 1179652
  7.2 127.6 %all-gather.2.cloned.1.call-start = ((), (), s32[]{:S(2)}) async-start(), calls=%async_computation.1 | async-start | bytes 1081344 | tf_op jit(solution)/shard_map/all_gather | solution.py:110
  7.9 293.1 %reduce-scatter.4.cloned.1.call-start = ((), (), s32[]{:S(2)}) async-start(), calls=%async_computation.3 | async-start | bytes 2162688
  164.0 331.4 %all-reduce.6.cloned.1.call-start = ((), (), s32[]{:S(2)}) async-start(), calls=%async_computation.2 | async-start | bytes 524288 | tf_op jit(solution)/shard_map/psum | solution.py:133
Sparse Core Ops, SparseCore 0:
  10.7 124.0 all-gather.1
  164.2 136.8 reduce-scatter.3
  304.6 190.7 all-reduce.5
where the time goes:
time: 504 us
  waiting for transfers between devices  456 us (90%)
  between operations  13.8 us (3%)
  local copies, waits for them, and re-layouts  11.7 us (2%)
  other arithmetic  9.99 us (2%)
  matrix products  7.03 us (1%)
    psum x1, waiting for transfers between devices, shards(): summed = lax.psum(shard_rows, 'dp')  193 us
    unnamed x4, waiting for transfers between devices  138 us
    all_gather x1, waiting for transfers between devices, shards(): lax.all_gather(query_weight, 'fsdp', axis=0, tiled=True)  126 us
  transfers between devices with their start and end apart: 3, of which 3 were waited for; matrix products, arithmetic and copies ran while one was open for 0% of the time, Pallas kernels for 0%

commit v1 on v0

v1 whole, which is shorter than its diff:
```python
import functools
import math

import jax
import jax.numpy as jnp
from jax import lax
from jax.experimental import pallas as pl
from jax.experimental.pallas import tpu as pltpu
from jax.sharding import PartitionSpec as P

MESH = pl.DeviceIdType.MESH
HEADS = 4
DEPTH = 128
SLOTS = 3
SPAN = 128
ROWS = SLOTS * SPAN
WIDTH = HEADS * DEPTH
MODEL = 1024
CHIPS = 16
PLANE = 32
RING = 32
EPSILON = 1e-06
SCALE = 1.0 / math.sqrt(DEPTH)
F32 = jnp.float32
BF16 = jnp.bfloat16


def dot(a, b, ca, cb):
    return lax.dot_general(a, b, (((ca,), (cb,)), ((), ())), preferred_element_type=F32)


def layer_kernel(
    total_seqs,
    events_hbm, weight_hbm, keys_hbm, values_hbm, gates_hbm, upstream_hbm, lengths_hbm,
    grad_keys_hbm, grad_values_hbm, grad_gates_hbm, grad_weight_ref,
    ev, kk, vv, gg, uu, lens,
    wf, wun, evt, gn, qq, att, dact, gm, gs, gq, out_k, out_v, out_g,
    gbuf, cbuf, sbuf, rbuf, tbuf, zbuf, gw,
    in_sem, near_s, near_r, rel_s, rel_r, agn_s, agn_r, agf_s, agf_r, cw_s, cw_r,
    cg_s, cg_r, rs_s, rs_r, zr_s, zr_r, fin_s, fin_r, out_sem,
):
    dp = lax.axis_index("dp")
    z = lax.axis_index("fsdp")
    core = lax.rem(dp, 2)
    chip = dp // 2
    x = chip // 4
    y = lax.rem(chip, 4)
    phase = lax.rem(y - z + RING, 4)
    is_source = lax.rem(z, 4) == y

    def ring_at(offset):
        return {"dp": dp, "fsdp": lax.rem(z + offset + RING, RING)}

    def chip_at(other, other_core):
        return {"dp": other * 2 + other_core, "fsdp": z}

    def remote(src, dst, ssem, rsem, device):
        return pltpu.make_async_remote_copy(
            src_ref=src, dst_ref=dst, send_sem=ssem, recv_sem=rsem,
            device_id=device, device_id_type=MESH,
        )

    partner = chip_at(chip, 1 - core)

    loads = [
        pltpu.make_async_copy(src, dst, in_sem.at[i])
        for i, (src, dst) in enumerate(
            (
                (lengths_hbm, lens), (gates_hbm, gg), (upstream_hbm, uu),
                (events_hbm, ev), (keys_hbm, kk), (values_hbm, vv),
            )
        )
    ]
    for load in loads:
        load.start()

    barrier = pltpu.get_barrier_semaphore()

    def tell(device):
        pl.semaphore_signal(barrier, inc=1, device_id=device, device_id_type=MESH)

    for j in (-2, -1, 1):
        tell(ring_at(phase + 4 * j))

    @pl.when(phase != 0)
    def _():
        tell(ring_at(phase))

    tell(ring_at(8))
    tell(ring_at(-8))
    for i in range(1, CHIPS):
        tell(chip_at(lax.rem(chip + i, CHIPS), core))
    tell(partner)
    pl.semaphore_wait(barrier, jnp.where(is_source, 33, 18))

    tile = weight_hbm.at[pl.ds(pl.multiple_of(core * 16, 16), 16), pl.ds(pl.multiple_of(x * 128, 128), 128)]
    own_tile = pltpu.make_async_copy(tile, wf.at[2, 0, core, x], near_r.at[2])
    near_sends = []
    for e in range(-7, 9):
        if e != 0:
            t = 8 - e
            near_sends.append(
                remote(tile, wf.at[t // 4, t % 4, core, x], near_s.at[t], near_r.at[t // 4], ring_at(e))
            )

    @pl.when(is_source)
    def _():
        for send in near_sends:
            send.start()
        own_tile.start()

    row_ids = lax.broadcasted_iota(jnp.int32, (SPAN, DEPTH), 0)
    col_ids = lax.broadcasted_iota(jnp.int32, (SPAN, DEPTH), 1)
    loads[0].wait()
    loads[1].wait()
    loads[2].wait()
    first_seq = (dp * RING + z) * SLOTS
    own_lens = [lens[first_seq + b] for b in range(SLOTS)]
    for b in range(SLOTS):
        rows = pl.ds(b * SPAN, SPAN)
        valid = row_ids < own_lens[b]
        parts = []
        for h in range(HEADS):
            cols = pl.ds(h * DEPTH, DEPTH)
            product = uu[rows, cols].astype(F32) * gg[rows, cols].astype(F32)
            parts.append(jnp.where(valid, product, 0.0))
        mean = jnp.sum(parts[0] + parts[1] + parts[2] + parts[3], axis=1, keepdims=True) * (1.0 / WIDTH)
        for h in range(HEADS):
            gn[rows, pl.ds(h * DEPTH, DEPTH)] = parts[h] - mean

    def near_arrived(jj):
        here = wf.at[jj, phase, core, x]
        remote(here, here, near_s.at[0], near_r.at[jj], partner).wait_recv()

    near_arrived(2)
    near_arrived(3)
    relay_down = remote(
        wf.at[pl.ds(2, 2), phase, core, x], wf.at[pl.ds(4, 2), phase, core, x], rel_s.at[0], rel_r.at[0], ring_at(-8)
    )
    relay_down.start()
    near_arrived(0)
    near_arrived(1)
    relay_up = remote(
        wf.at[pl.ds(0, 2), phase, core, x], wf.at[pl.ds(6, 2), phase, core, x], rel_s.at[1], rel_r.at[1], ring_at(8)
    )
    relay_up.start()

    def spread(first, ssem, rsem):
        piece = wf.at[pl.ds(first, 4), phase, core, x]
        sends = [
            remote(piece, piece, ssem.at[i], rsem.at[i], chip_at(lax.rem(chip + i, CHIPS), core))
            for i in range(1, CHIPS)
        ]
        for send in sends:
            send.start()
        return sends

    def gathered(first, ssem, rsem):
        for i in range(1, CHIPS):
            other = lax.rem(chip - i + CHIPS, CHIPS)
            there = wf.at[pl.ds(first, 4), lax.rem(lax.rem(other, 4) - z + RING, 4), core, other // 4]
            remote(there, there, ssem.at[i], rsem.at[i], partner).wait_recv()

    near_spread = spread(0, agn_s, agn_r)
    loads[3].wait()
    for m in range(0, MODEL, 128):
        evt[pl.ds(m, 128), :] = ev[:, pl.ds(m, 128)].T
    relay_down.wait_recv()
    relay_up.wait_recv()
    far_spread = spread(4, agf_s, agf_r)
    gathered(0, agn_s, agn_r)
    swaps = []

    def swap(first, index):
        mine = wf.at[pl.ds(first, 4), :, core]
        copy = remote(mine, mine, cw_s.at[index], cw_r.at[index], partner)
        copy.start()
        swaps.append(copy)

    swap(0, 0)
    gathered(4, agf_s, agf_r)
    swap(4, 1)
    loads[4].wait()
    loads[5].wait()
    swaps[0].wait_recv()
    swaps[1].wait_recv()

    for shard in range(RING):
        t = lax.rem(shard - z + 8 + RING, RING)
        for half in range(2):
            for c in range(4):
                wun[pl.ds(shard * 32 + half * 16, 16), pl.ds(c * 128, 128)] = wf[t // 4, lax.rem(t, 4), half, c]

    qq[...] = dot(ev[...], wun[...], 1, 0).astype(BF16)
    for b in range(SLOTS):
        rows = pl.ds(b * SPAN, SPAN)
        inverse = 1.0 / jnp.full((1, DEPTH), own_lens[b].astype(F32))
        weight = jnp.where((col_ids <= row_ids) & (row_ids < own_lens[b]), inverse, 0.0)
        mixed = []
        for h in range(HEADS):
            cols = pl.ds(h * DEPTH, DEPTH)
            scores = dot(qq[rows, cols], kk[rows, cols], 1, 1) * SCALE
            sigmoid = 0.5 * jnp.tanh(0.5 * scores) + 0.5
            weighted = sigmoid * weight
            attention = (scores * weighted).astype(BF16)
            att[b * HEADS + h] = attention
            dact[b * HEADS + h] = weighted * (1.0 + scores * (1.0 - sigmoid))
            mixed.append(dot(attention, vv[rows, cols], 1, 0))
        mean = jnp.sum(mixed[0] + mixed[1] + mixed[2] + mixed[3], axis=1, keepdims=True) * (1.0 / WIDTH)
        centred = [m - mean for m in mixed]
        squares = [m * m for m in centred]
        var = jnp.sum(squares[0] + squares[1] + squares[2] + squares[3], axis=1, keepdims=True) * (1.0 / WIDTH)
        inv_std = lax.rsqrt(var + EPSILON)
        normed = [m * inv_std for m in centred]
        grads = [gn[rows, pl.ds(h * DEPTH, DEPTH)] for h in range(HEADS)]
        overlap = [g * n for g, n in zip(grads, normed)]
        slope = jnp.sum(overlap[0] + overlap[1] + overlap[2] + overlap[3], axis=1, keepdims=True) * (1.0 / WIDTH)
        for h in range(HEADS):
            cols = pl.ds(h * DEPTH, DEPTH)
            gm[rows, cols] = (inv_std * (grads[h] - normed[h] * slope)).astype(BF16)
            out_g[rows, cols] = (uu[rows, cols].astype(F32) * normed[h]).astype(BF16)

    core_sends = []
    rs_sends = []

    def reduce_head(h):
        core_sends[h].wait_recv()
        summed = gbuf[h, :, :, core].astype(F32) + cbuf[h].astype(F32)
        sbuf[h] = summed.astype(BF16)
        for r in range(4):
            target = ((h - r) % 4) * 4 + r
            send = remote(
                sbuf.at[h, :, r], rbuf.at[chip], rs_s.at[h * 4 + r], rs_r.at[chip], chip_at(target, core)
            )
            rs_sends.append((target, send))

            @pl.when(chip != target)
            def _():
                send.start()

    for h in range(HEADS):
        cols = pl.ds(h * DEPTH, DEPTH)
        for b in range(SLOTS):
            rows = pl.ds(b * SPAN, SPAN)
            grad_attention = dot(gm[rows, cols], vv[rows, cols], 1, 1)
            grad_scores = (grad_attention * dact[b * HEADS + h]).astype(BF16)
            gs[b * HEADS + h] = grad_scores
            gq[rows, :] = (dot(grad_scores, kk[rows, cols], 1, 0) * SCALE).astype(BF16)
        gbuf[h] = dot(evt[...], gq[...], 1, 0).astype(BF16).reshape(8, 4, 2, 16, 128)
        send = remote(gbuf.at[h, :, :, 1 - core], cbuf.at[h], cg_s.at[h], cg_r.at[h], partner)
        send.start()
        core_sends.append(send)
        if h > 0:
            reduce_head(h - 1)
    reduce_head(HEADS - 1)

    head = lax.rem(x + y, 4)
    total = sbuf[head, :, y].astype(F32)
    for i in range(1, CHIPS):
        other = lax.rem(chip + i, CHIPS)
        there = rbuf.at[other]
        remote(there, there, rs_s.at[0], rs_r.at[other], partner).wait_recv()
        total = total + rbuf[other].astype(F32)
    tbuf[...] = total.astype(BF16)
    ring_sends = []
    for k in range(8):
        target = 4 * k + y
        send = remote(tbuf.at[k], zbuf.at[z], zr_s.at[k], zr_r.at[z], {"dp": dp, "fsdp": target})
        ring_sends.append((target, send))

        @pl.when(target != z)
        def _():
            send.start()

    for b in range(SLOTS):
        rows = pl.ds(b * SPAN, SPAN)
        for h in range(HEADS):
            cols = pl.ds(h * DEPTH, DEPTH)
            out_v[rows, cols] = dot(att[b * HEADS + h], gm[rows, cols], 0, 0).astype(BF16)
            out_k[rows, cols] = (dot(gs[b * HEADS + h], qq[rows, cols], 0, 0) * SCALE).astype(BF16)
    stores = [
        pltpu.make_async_copy(src, dst, out_sem.at[i])
        for i, (src, dst) in enumerate(((out_k, grad_keys_hbm), (out_v, grad_values_hbm), (out_g, grad_gates_hbm)))
    ]
    for store in stores:
        store.start()

    final_sends = []
    for i in range(1, PLANE):
        there = gw.at[core, head]
        final_sends.append(
            remote(there, there, fin_s.at[i], fin_r.at[x * 2 + core], {"dp": lax.rem(dp + i, PLANE), "fsdp": z})
        )

    @pl.when(is_source)
    def _():
        acc = tbuf[z // 4].astype(F32)
        for i in range(1, RING):
            other = lax.rem(z + i, RING)
            there = zbuf.at[other]
            remote(there, there, zr_s.at[0], zr_r.at[other], partner).wait_recv()
            acc = acc + zbuf[other].astype(F32)
        gw[core, head] = acc * (1.0 / total_seqs)
        for send in final_sends:
            send.start()

    source_y = lax.rem(z, 4)
    for sx in range(4):
        for sc in range(2):
            @pl.when((chip != sx * 4 + source_y) | (core != sc))
            def _():
                there = gw.at[sc, lax.rem(sx + source_y, 4)]
                remote(there, there, fin_s.at[0], fin_r.at[sx * 2 + sc], partner).wait_recv()
    for half in range(2):
        for h in range(HEADS):
            grad_weight_ref[pl.ds(half * 16, 16), pl.ds(h * DEPTH, DEPTH)] = gw[half, h]

    @pl.when(is_source)
    def _():
        for send in near_sends:
            send.wait_send()
        for send in final_sends:
            send.wait_send()

    relay_down.wait_send()
    relay_up.wait_send()
    for send in near_spread + far_spread + swaps + core_sends:
        send.wait_send()
    for target, send in rs_sends:
        @pl.when(chip != target)
        def _():
            send.wait_send()
    for target, send in ring_sends:
        @pl.when(target != z)
        def _():
            send.wait_send()
    for store in stores:
        store.wait()


def shards(events, query_weight, keys, values, gates, cotangent, lengths):
    flat = [a.reshape(ROWS, a.shape[2]) for a in (events, keys, values, gates, cotangent)]
    hbm = pl.BlockSpec(memory_space=pl.ANY)
    vmem = pltpu.VMEM
    dma = pltpu.SemaphoreType.DMA
    row_out = jax.ShapeDtypeStruct((ROWS, WIDTH), BF16)
    scratch = [
        vmem((ROWS, MODEL), BF16), vmem((ROWS, WIDTH), BF16), vmem((ROWS, WIDTH), BF16),
        vmem((ROWS, WIDTH), BF16), vmem((ROWS, WIDTH), BF16), pltpu.SMEM(lengths.shape, jnp.int32),
        vmem((8, 4, 2, 4, 16, 128), BF16), vmem((MODEL, WIDTH), BF16), vmem((MODEL, ROWS), BF16),
        vmem((ROWS, WIDTH), F32), vmem((ROWS, WIDTH), BF16), vmem((12, SPAN, SPAN), BF16),
        vmem((12, SPAN, SPAN), F32), vmem((ROWS, WIDTH), BF16), vmem((12, SPAN, SPAN), BF16),
        vmem((ROWS, DEPTH), BF16),
        vmem((ROWS, WIDTH), BF16), vmem((ROWS, WIDTH), BF16), vmem((ROWS, WIDTH), BF16),
        vmem((4, 8, 4, 2, 16, 128), BF16), vmem((4, 8, 4, 16, 128), BF16), vmem((4, 8, 4, 16, 128), BF16),
        vmem((16, 8, 16, 128), BF16), vmem((8, 16, 128), BF16), vmem((RING, 16, 128), BF16),
        vmem((2, 4, 16, 128), F32),
        dma((6,)), dma((16,)), dma((4,)), dma((2,)), dma((2,)), dma((16,)), dma((16,)), dma((16,)), dma((16,)),
        dma((2,)), dma((2,)), dma((4,)), dma((4,)), dma((16,)), dma((16,)), dma((8,)), dma((32,)),
        dma((32,)), dma((8,)), dma((3,)),
    ]
    grad_keys, grad_values, grad_gates, grad_weight = pl.pallas_call(
        functools.partial(layer_kernel, lengths.shape[0]),
        out_shape=(row_out, row_out, row_out, jax.ShapeDtypeStruct((32, WIDTH), F32)),
        in_specs=[hbm] * 7,
        out_specs=(hbm, hbm, hbm, pl.BlockSpec(memory_space=vmem)),
        scratch_shapes=scratch,
        compiler_params=pltpu.CompilerParams(
            collective_id=0, has_side_effects=True, vmem_limit_bytes=48 * 2**20
        ),
        name="layer",
    )(flat[0], query_weight, flat[1], flat[2], flat[3], flat[4], lengths)
    shape = keys.shape
    return grad_keys.reshape(shape), grad_values.reshape(shape), grad_gates.reshape(shape), grad_weight


def solution(mesh):
    by_seq = P(("dp", "fsdp"), None, None)
    return jax.shard_map(
        shards,
        mesh=mesh,
        in_specs=(by_seq, P("fsdp", None), by_seq, by_seq, by_seq, by_seq, P()),
        out_specs=(by_seq, by_seq, by_seq, P("fsdp", None)),
        check_vma=False,
    )
```

time: 504 us -> 90.1 us (0.18)
  waiting for transfers between devices: 456 us -> 0 us
  Pallas kernels: 0 us -> 79.6 us
  between operations: 13.8 us -> 0.66 us
  other arithmetic: 9.99 us -> 0 us
  matrix products: 7.03 us -> 0 us
    psum x1 -> x0, waiting for transfers between devices: 193 us -> none  [shards(): summed = lax.psum(shard_rows, 'dp')]
    unnamed x4 -> x0, waiting for transfers between devices: 138 us -> none
    all_gather x1 -> x0, waiting for transfers between devices: 126 us -> none  [shards(): lax.all_gather(query_weight, 'fsdp', axis=0, tiled=True)]
    pallas_call x0 -> x1, Pallas kernels: none -> 79.6 us  [shards(): pl.pallas_call(functools.partial(layer_kernel, lengths.shape[0]), out_sha...]
    dot_general x20 -> x0, matrix products: 7.03 us -> none  [the longest x1 1.79 us: shards(): jnp.dot(columns, lax.all_gather(query_weight, 'fsdp', axis=0, tiled=True)...]
    unnamed x9 -> x18, local copies, waits for them, and re-layouts: 4.3 us -> 9.44 us
  transfers between devices with their start and end apart: 3 -> 0, of which waited for: 3 -> 0; matrix products, arithmetic and copies ran while one was open for 0% -> 0% of each run, Pallas kernels for 0% -> 0%
where the time goes in v1:
time: 90.1 us; the launch traced here: 89.7 us
  Pallas kernels  79.6 us (88%)
  local copies, waits for them, and re-layouts  9.44 us (10%)
    pallas_call x1, Pallas kernels, shards(): pl.pallas_call(functools.partial(layer_kernel, lengths.shape[0]), out_sha...  79.6 us
    unnamed x18, local copies, waits for them, and re-layouts  9.44 us

profile of v1, /device:TPU:1, one launch (start us, length us, event | category | flops | bytes accessed | tf_op | source)
XLA Modules:
  0.0 89.7 jit_solution(5598369482774626995)
XLA Ops:
  0.6 0.0 copy-start
  0.6 1.1 %copy-done = bf16[3,128,1024]{2,1,0:T(8,128)(2,1)S(1)} copy-done((bf16[3,128,1024]{2,1,0:T(8,128)(2,1)S(1)}, bf16[3,128,1024]{2,1,0:T(8,128)(2,1)}, u32[]{:S(2)}) %copy-start) | copy-done | bytes 786456
  1.8 0.0 copy-start.1
  1.8 1.0 %copy-done.1 = bf16[3,128,512]{2,1,0:T(8,128)(2,1)S(1)} copy-done((bf16[3,128,512]{2,1,0:T(8,128)(2,1)S(1)}, bf16[3,128,512]{2,1,0:T(8,128)(2,1)}, u32[]{:S(2)}) %copy-start.1) | copy-done | bytes 393240
  2.8 0.0 copy-start.2
  2.8 1.0 %copy-done.2 = bf16[3,128,512]{2,1,0:T(8,128)(2,1)S(1)} copy-done((bf16[3,128,512]{2,1,0:T(8,128)(2,1)S(1)}, bf16[3,128,512]{2,1,0:T(8,128)(2,1)}, u32[]{:S(2)}) %copy-start.2) | copy-done | bytes 393240
  3.8 0.0 copy-start.3
  3.8 1.0 %copy-done.3 = bf16[3,128,512]{2,1,0:T(8,128)(2,1)S(1)} copy-done((bf16[3,128,512]{2,1,0:T(8,128)(2,1)S(1)}, bf16[3,128,512]{2,1,0:T(8,128)(2,1)}, u32[]{:S(2)}) %copy-start.3) | copy-done | bytes 393240
  4.8 0.0 copy-start.4
  4.8 1.0 %copy-done.4 = bf16[3,128,512]{2,1,0:T(8,128)(2,1)S(1)} copy-done((bf16[3,128,512]{2,1,0:T(8,128)(2,1)S(1)}, bf16[3,128,512]{2,1,0:T(8,128)(2,1)}, u32[]{:S(2)}) %copy-start.4) | copy-done | bytes 393240
  5.8 0.0 copy-start.5
  5.8 0.8 copy-done.5
  6.5 0.0 copy-start.6
  6.5 0.7 copy-done.6
  7.2 79.6 %layer.1 = (bf16[384,512]{1,0:T(8,128)(2,1)S(1)}, bf16[384,512]{1,0:T(8,128)(2,1)S(1)}, bf16[384,512]{1,0:T(8,128)(2,1)S(1)}, f32[32,512]{1,0:T(8,128)S(1)}) custom-call(bf16[384,1024]{1,0:T(8,128)(2,1)S(1)} %bitcast.8, bf16[32,512]{1,0:T(8,128)(2,1)S(1)} %copy-done.5, bf16[384,512]{1,0:T(8,128)(2,1)S(1)} %bitcast.9, bf16[384,512]{1,0:T(8,128)(2,1)S(1)} %bitcast.10, ...), custom_call_target="tpu_custom_call" | custom-call | tf_op jit(solution)/shard_map/layer/pallas_call | solution.py:362
  86.8 0.7 copy.15
  87.6 0.7 copy.16
  88.3 0.7 copy.17
  89.1 0.6 copy.18
Async XLA Ops:
  0.6 1.1 %copy-start = (bf16[3,128,1024]{2,1,0:T(8,128)(2,1)S(1)}, bf16[3,128,1024]{2,1,0:T(8,128)(2,1)}, u32[]{:S(2)}) copy-start(bf16[3,128,1024]{2,1,0:T(8,128)(2,1)} %param.7) | copy-start | bytes 2359300
  1.8 1.0 %copy-start.1 = (bf16[3,128,512]{2,1,0:T(8,128)(2,1)S(1)}, bf16[3,128,512]{2,1,0:T(8,128)(2,1)}, u32[]{:S(2)}) copy-start(bf16[3,128,512]{2,1,0:T(8,128)(2,1)} %param.9) | copy-start | bytes 1179652
  2.8 1.0 %copy-start.2 = (bf16[3,128,512]{2,1,0:T(8,128)(2,1)S(1)}, bf16[3,128,512]{2,1,0:T(8,128)(2,1)}, u32[]{:S(2)}) copy-start(bf16[3,128,512]{2,1,0:T(8,128)(2,1)} %param.10) | copy-start | bytes 1179652
  3.8 1.0 %copy-start.3 = (bf16[3,128,512]{2,1,0:T(8,128)(2,1)S(1)}, bf16[3,128,512]{2,1,0:T(8,128)(2,1)}, u32[]{:S(2)}) copy-start(bf16[3,128,512]{2,1,0:T(8,128)(2,1)} %param.11) | copy-start | bytes 1179652
  4.8 1.0 %copy-start.4 = (bf16[3,128,512]{2,1,0:T(8,128)(2,1)S(1)}, bf16[3,128,512]{2,1,0:T(8,128)(2,1)}, u32[]{:S(2)}) copy-start(bf16[3,128,512]{2,1,0:T(8,128)(2,1)} %param.12) | copy-start | bytes 1179652
  5.8 0.8 copy-start.5
  6.5 0.7 copy-start.6

commit v2 on v1

v2 whole, which is shorter than its diff:
```python
import functools
import math

import jax
import jax.numpy as jnp
from jax import lax
from jax.experimental import pallas as pl
from jax.experimental.pallas import tpu as pltpu
from jax.sharding import PartitionSpec as P

MESH = pl.DeviceIdType.MESH
HEADS = 4
DEPTH = 128
SLOTS = 3
SPAN = 128
ROWS = SLOTS * SPAN
WIDTH = HEADS * DEPTH
MODEL = 1024
CHIPS = 16
RING = 32
EPSILON = 1e-06
SCALE = 1.0 / math.sqrt(DEPTH)
F32 = jnp.float32
BF16 = jnp.bfloat16


OTHER_CHIPS = sorted(
    ((i // 4, i % 4) for i in range(1, CHIPS)), key=lambda d: -(min(d[0], 4 - d[0]) + min(d[1], 4 - d[1]))
)
PLACES = (0, -1, 1, -2, 2, -3, 3, -4)


def dot(a, b, ca, cb):
    return lax.dot_general(a, b, (((ca,), (cb,)), ((), ())), preferred_element_type=F32)


def layer_kernel(
    total_seqs,
    events_hbm, weight_hbm, keys_hbm, values_hbm, gates_hbm, upstream_hbm, lengths_hbm,
    grad_keys_hbm, grad_values_hbm, grad_gates_hbm, grad_weight_ref,
    ev, kk, vv, gg, uu, lens,
    wf, wun, evt, gn, qq, att, dact, gm, gs, gq, out_k, out_v, out_g,
    gbuf, cbuf, sbuf, rbuf, tbuf, zbuf, gw,
    in_sem, near_s, near_r, rel_s, rel_r, ag_s, ag_r, cw_s, cw_r,
    cg_s, cg_r, rs_s, rs_r, zr_s, zr_r, fin_s, fin_r, out_sem,
):
    dp = lax.axis_index("dp")
    z = lax.axis_index("fsdp")
    core = lax.rem(dp, 2)
    chip = dp // 2
    x = chip // 4
    y = lax.rem(chip, 4)
    phase = lax.rem(y - z + RING, 4)
    is_source = lax.rem(z, 4) == y

    def ring_at(offset):
        return {"dp": dp, "fsdp": lax.rem(z + offset + RING, RING)}

    def chip_at(dx, dy, other_core):
        return {"dp": (lax.rem(x + dx, 4) * 4 + lax.rem(y + dy, 4)) * 2 + other_core, "fsdp": z}

    def remote(src, dst, ssem, rsem, device):
        return pltpu.make_async_remote_copy(
            src_ref=src, dst_ref=dst, send_sem=ssem, recv_sem=rsem,
            device_id=device, device_id_type=MESH,
        )

    partner = chip_at(0, 0, 1 - core)

    barrier = pltpu.get_barrier_semaphore()

    def tell(device):
        pl.semaphore_signal(barrier, inc=1, device_id=device, device_id_type=MESH)

    tell(ring_at(8))
    tell(ring_at(-8))
    for j in (-2, 1, -1):
        tell(ring_at(phase + 4 * j))

    @pl.when(phase != 0)
    def _():
        tell(ring_at(phase))

    for dx, dy in OTHER_CHIPS:
        tell(chip_at(dx, dy, core))
    tell(partner)
    loads = [
        pltpu.make_async_copy(src, dst, in_sem.at[i])
        for i, (src, dst) in enumerate(
            (
                (lengths_hbm, lens), (gates_hbm, gg), (upstream_hbm, uu),
                (events_hbm, ev), (keys_hbm, kk), (values_hbm, vv),
            )
        )
    ]
    for load in loads:
        load.start()

    pl.semaphore_wait(barrier, jnp.where(is_source, 33, 18))

    tile = weight_hbm.at[pl.ds(pl.multiple_of(core * 16, 16), 16), pl.ds(pl.multiple_of(x * 128, 128), 128)]
    own_tile = pltpu.make_async_copy(tile, wf.at[0, 0, core, x], near_r.at[0])
    near_sends = []
    for e in (8, -7, 7, -6, 6, -5, 5, -4, 4, -3, 3, -2, 2, -1, 1):
        ring_class = -e % 4
        place = PLACES.index((-e - ring_class) // 4)
        near_sends.append(
            remote(tile, wf.at[place, ring_class, core, x], near_s.at[e + 7], near_r.at[place], ring_at(e))
        )

    @pl.when(is_source)
    def _():
        for send in near_sends:
            send.start()
        own_tile.start()

    row_ids = lax.broadcasted_iota(jnp.int32, (SPAN, DEPTH), 0)
    col_ids = lax.broadcasted_iota(jnp.int32, (SPAN, DEPTH), 1)
    loads[0].wait()
    loads[1].wait()
    loads[2].wait()
    first_seq = (dp * RING + z) * SLOTS
    own_lens = [lens[first_seq + b] for b in range(SLOTS)]
    for b in range(SLOTS):
        rows = pl.ds(b * SPAN, SPAN)
        valid = row_ids < own_lens[b]
        parts = []
        for h in range(HEADS):
            cols = pl.ds(h * DEPTH, DEPTH)
            product = uu[rows, cols].astype(F32) * gg[rows, cols].astype(F32)
            parts.append(jnp.where(valid, product, 0.0))
        mean = jnp.sum(parts[0] + parts[1] + parts[2] + parts[3], axis=1, keepdims=True) * (1.0 / WIDTH)
        for h in range(HEADS):
            gn[rows, pl.ds(h * DEPTH, DEPTH)] = parts[h] - mean

    relays = []

    def relay(place):
        here = wf.at[place, phase, core, x]
        remote(here, here, near_s.at[0], near_r.at[place], partner).wait_recv()
        copy = remote(
            here, wf.at[place + 4, phase, core, x], rel_s.at[place], rel_r.at[place], ring_at(8 if place % 2 else -8)
        )
        copy.start()
        relays.append(copy)

    spreads = []

    def spread(group):
        piece = wf.at[pl.ds(2 * group, 2), phase, core, x]
        for dx, dy in OTHER_CHIPS:
            i = group * CHIPS + dx * 4 + dy
            send = remote(piece, piece, ag_s.at[i], ag_r.at[i], chip_at(dx, dy, core))
            send.start()
            spreads.append(send)

    swaps = []

    def swap(group):
        for dx, dy in reversed(OTHER_CHIPS):
            i = group * CHIPS + dx * 4 + dy
            other_class = lax.rem(lax.rem(y + 4 - dy, 4) - z + RING, 4)
            there = wf.at[pl.ds(2 * group, 2), other_class, core, lax.rem(x + 4 - dx, 4)]
            remote(there, there, ag_s.at[i], ag_r.at[i], partner).wait_recv()
        mine = wf.at[pl.ds(2 * group, 2), :, core]
        copy = remote(mine, mine, cw_s.at[group], cw_r.at[group], partner)
        copy.start()
        swaps.append(copy)

    def unpack(group):
        swaps[group].wait_recv()
        for place in (2 * group, 2 * group + 1):
            for ring_class in range(4):
                shard = lax.rem(z + ring_class + 4 * PLACES[place] + RING, RING)
                for half in range(2):
                    for c in range(4):
                        wun[shard, half, :, pl.ds(c * 128, 128)] = wf[place, ring_class, half, c]

    relay(0)
    relay(1)
    spread(0)
    relay(2)
    relay(3)
    spread(1)
    loads[3].wait()
    for m in range(0, MODEL, 128):
        evt[pl.ds(m, 128), :] = ev[:, pl.ds(m, 128)].T
    relays[0].wait_recv()
    relays[1].wait_recv()
    spread(2)
    swap(0)
    swap(1)
    relays[2].wait_recv()
    relays[3].wait_recv()
    spread(3)
    unpack(0)
    swap(2)
    unpack(1)
    loads[4].wait()
    loads[5].wait()
    swap(3)
    unpack(2)
    unpack(3)

    qq[...] = dot(ev[...], wun[...].reshape(MODEL, WIDTH), 1, 0).astype(BF16)
    for b in range(SLOTS):
        rows = pl.ds(b * SPAN, SPAN)
        inverse = 1.0 / jnp.full((1, DEPTH), own_lens[b].astype(F32))
        weight = jnp.where((col_ids <= row_ids) & (row_ids < own_lens[b]), inverse, 0.0)
        mixed = []
        for h in range(HEADS):
            cols = pl.ds(h * DEPTH, DEPTH)
            scores = dot(qq[rows, cols], kk[rows, cols], 1, 1) * SCALE
            sigmoid = 0.5 * jnp.tanh(0.5 * scores) + 0.5
            weighted = sigmoid * weight
            attention = (scores * weighted).astype(BF16)
            att[b * HEADS + h] = attention
            dact[b * HEADS + h] = weighted * (1.0 + scores * (1.0 - sigmoid))
            mixed.append(dot(attention, vv[rows, cols], 1, 0))
        mean = jnp.sum(mixed[0] + mixed[1] + mixed[2] + mixed[3], axis=1, keepdims=True) * (1.0 / WIDTH)
        centred = [m - mean for m in mixed]
        squares = [m * m for m in centred]
        var = jnp.sum(squares[0] + squares[1] + squares[2] + squares[3], axis=1, keepdims=True) * (1.0 / WIDTH)
        inv_std = lax.rsqrt(var + EPSILON)
        normed = [m * inv_std for m in centred]
        grads = [gn[rows, pl.ds(h * DEPTH, DEPTH)] for h in range(HEADS)]
        overlap = [g * n for g, n in zip(grads, normed)]
        slope = jnp.sum(overlap[0] + overlap[1] + overlap[2] + overlap[3], axis=1, keepdims=True) * (1.0 / WIDTH)
        for h in range(HEADS):
            cols = pl.ds(h * DEPTH, DEPTH)
            gm[rows, cols] = (inv_std * (grads[h] - normed[h] * slope)).astype(BF16)
            out_g[rows, cols] = (uu[rows, cols].astype(F32) * normed[h]).astype(BF16)

    core_sends = []
    rs_sends = []

    def reduce_head(h):
        core_sends[h].wait_recv()
        summed = gbuf[h, :, :, core].astype(F32) + cbuf[h].astype(F32)
        sbuf[h] = summed.astype(BF16)
        for dx, dy in OTHER_CHIPS:
            there_x, there_y = lax.rem(x + dx, 4), lax.rem(y + dy, 4)
            i = h * CHIPS + dx * 4 + dy
            send = remote(
                sbuf.at[h, pl.ds(2 * lax.rem(there_x + h, 4), 2), there_y], rbuf.at[chip, h],
                rs_s.at[i], rs_r.at[i], chip_at(dx, dy, core),
            )
            send.start()
            rs_sends.append(send)

    for h in range(HEADS):
        cols = pl.ds(h * DEPTH, DEPTH)
        for b in range(SLOTS):
            rows = pl.ds(b * SPAN, SPAN)
            grad_attention = dot(gm[rows, cols], vv[rows, cols], 1, 1)
            grad_scores = (grad_attention * dact[b * HEADS + h]).astype(BF16)
            gs[b * HEADS + h] = grad_scores
            gq[rows, :] = (dot(grad_scores, kk[rows, cols], 1, 0) * SCALE).astype(BF16)
        gbuf[h] = dot(evt[...], gq[...], 1, 0).astype(BF16).reshape(8, 4, 2, 16, 128)
        send = remote(gbuf.at[h, :, :, 1 - core], cbuf.at[h], cg_s.at[h], cg_r.at[h], partner)
        send.start()
        core_sends.append(send)
        if h > 0:
            reduce_head(h - 1)
    reduce_head(HEADS - 1)

    ring_sends = []
    for h in range(HEADS):
        pair = lax.rem(x + h, 4)
        total = sbuf[h, pl.ds(2 * pair, 2), y].astype(F32)
        for dx, dy in reversed(OTHER_CHIPS):
            i = h * CHIPS + dx * 4 + dy
            other = lax.rem(x + 4 - dx, 4) * 4 + lax.rem(y + 4 - dy, 4)
            there = rbuf.at[other, h]
            remote(there, there, rs_s.at[i], rs_r.at[i], partner).wait_recv()
            total = total + rbuf[other, h].astype(F32)
        tbuf[h] = total.astype(BF16)
        for k in range(2):
            target = 8 * pair + 4 * k + y
            send = remote(tbuf.at[h, k], zbuf.at[z], zr_s.at[2 * h + k], zr_r.at[z], {"dp": dp, "fsdp": target})
            ring_sends.append((target, send))

            @pl.when(target != z)
            def _():
                send.start()

    for b in range(SLOTS):
        rows = pl.ds(b * SPAN, SPAN)
        for h in range(HEADS):
            cols = pl.ds(h * DEPTH, DEPTH)
            out_v[rows, cols] = dot(att[b * HEADS + h], gm[rows, cols], 0, 0).astype(BF16)
            out_k[rows, cols] = (dot(gs[b * HEADS + h], qq[rows, cols], 0, 0) * SCALE).astype(BF16)
    stores = [
        pltpu.make_async_copy(src, dst, out_sem.at[i])
        for i, (src, dst) in enumerate(((out_k, grad_keys_hbm), (out_v, grad_values_hbm), (out_g, grad_gates_hbm)))
    ]
    for store in stores:
        store.start()

    head = lax.rem(z // 8 + 4 - x, 4)
    final_sends = []
    for dx, dy, swapped in [(dx, dy, k) for dx, dy in OTHER_CHIPS for k in range(2)] + [(0, 0, 1)]:
        there = gw.at[core, head]
        other_core = 1 - core if swapped else core
        final_sends.append(
            remote(
                there, there, fin_s.at[dx * 8 + dy * 2 + swapped], fin_r.at[x * 2 + core],
                chip_at(dx, dy, other_core),
            )
        )

    @pl.when(is_source)
    def _():
        acc = tbuf[head, lax.rem(z // 4, 2)].astype(F32)
        for i in range(1, RING):
            other = lax.rem(z + i, RING)
            there = zbuf.at[other]
            remote(there, there, zr_s.at[0], zr_r.at[other], partner).wait_recv()
            acc = acc + zbuf[other].astype(F32)
        gw[core, head] = (acc * (1.0 / total_seqs)).astype(BF16)
        for send in final_sends:
            send.start()

    source_y = lax.rem(z, 4)
    for sx in range(4):
        for sc in range(2):
            @pl.when((chip != sx * 4 + source_y) | (core != sc))
            def _():
                there = gw.at[sc, lax.rem(z // 8 + 4 - sx, 4)]
                remote(there, there, fin_s.at[0], fin_r.at[sx * 2 + sc], partner).wait_recv()
    for half in range(2):
        for h in range(HEADS):
            grad_weight_ref[pl.ds(half * 16, 16), pl.ds(h * DEPTH, DEPTH)] = gw[half, h].astype(F32)

    @pl.when(is_source)
    def _():
        for send in near_sends:
            send.wait_send()
        for send in final_sends:
            send.wait_send()

    for send in relays + spreads + swaps + core_sends + rs_sends:
        send.wait_send()
    for target, send in ring_sends:
        @pl.when(target != z)
        def _():
            send.wait_send()
    for store in stores:
        store.wait()


def store_kernel(*refs):
    count = (len(refs) - 2) // 3
    sources, results, held = refs[:count], refs[count : 2 * count], refs[2 * count : 3 * count]
    in_sem, out_sem = refs[-2:]
    loads = [pltpu.make_async_copy(a, b, in_sem.at[i]) for i, (a, b) in enumerate(zip(sources, held))]
    stores = [pltpu.make_async_copy(a, b, out_sem.at[i]) for i, (a, b) in enumerate(zip(held, results))]
    for load in loads:
        load.start()
    for load, store in zip(loads, stores):
        load.wait()
        store.start()
    for store in stores:
        store.wait()


def shards(events, query_weight, keys, values, gates, cotangent, lengths):
    flat = [a.reshape(ROWS, a.shape[2]) for a in (events, keys, values, gates, cotangent)]
    hbm = pl.BlockSpec(memory_space=pl.ANY)
    vmem = pltpu.VMEM
    dma = pltpu.SemaphoreType.DMA
    row_out = jax.ShapeDtypeStruct((ROWS, WIDTH), BF16)
    scratch = [
        vmem((ROWS, MODEL), BF16), vmem((ROWS, WIDTH), BF16), vmem((ROWS, WIDTH), BF16),
        vmem((ROWS, WIDTH), BF16), vmem((ROWS, WIDTH), BF16), pltpu.SMEM(lengths.shape, jnp.int32),
        vmem((8, 4, 2, 4, 16, 128), BF16), vmem((RING, 2, 16, WIDTH), BF16), vmem((MODEL, ROWS), BF16),
        vmem((ROWS, WIDTH), F32), vmem((ROWS, WIDTH), BF16), vmem((12, SPAN, SPAN), BF16),
        vmem((12, SPAN, SPAN), F32), vmem((ROWS, WIDTH), BF16), vmem((12, SPAN, SPAN), BF16),
        vmem((ROWS, DEPTH), BF16),
        vmem((ROWS, WIDTH), BF16), vmem((ROWS, WIDTH), BF16), vmem((ROWS, WIDTH), BF16),
        vmem((4, 8, 4, 2, 16, 128), BF16), vmem((4, 8, 4, 16, 128), BF16), vmem((4, 8, 4, 16, 128), BF16),
        vmem((16, 4, 2, 16, 128), BF16), vmem((4, 2, 16, 128), BF16), vmem((RING, 16, 128), BF16),
        vmem((2, 4, 16, 128), BF16),
        dma((6,)), dma((16,)), dma((4,)), dma((4,)), dma((4,)), dma((64,)), dma((64,)),
        dma((4,)), dma((4,)), dma((4,)), dma((4,)), dma((64,)), dma((64,)), dma((8,)), dma((32,)),
        dma((32,)), dma((8,)), dma((3,)),
    ]
    grad_keys, grad_values, grad_gates, grad_weight = pl.pallas_call(
        functools.partial(layer_kernel, lengths.shape[0]),
        out_shape=(row_out, row_out, row_out, jax.ShapeDtypeStruct((32, WIDTH), F32)),
        in_specs=[hbm] * 7,
        out_specs=(hbm, hbm, hbm, pl.BlockSpec(memory_space=vmem)),
        scratch_shapes=scratch,
        compiler_params=pltpu.CompilerParams(
            collective_id=0, has_side_effects=True, vmem_limit_bytes=60 * 2**20
        ),
        name="layer",
    )(flat[0], query_weight, flat[1], flat[2], flat[3], flat[4], lengths)
    results = (grad_keys, grad_values, grad_gates, grad_weight)
    grad_keys, grad_values, grad_gates, grad_weight = pl.pallas_call(
        store_kernel,
        out_shape=tuple(jax.ShapeDtypeStruct(r.shape, r.dtype) for r in results),
        in_specs=[hbm] * 4,
        out_specs=(hbm,) * 4,
        scratch_shapes=[vmem(r.shape, r.dtype) for r in results] + [dma((4,)), dma((4,))],
        compiler_params=pltpu.CompilerParams(vmem_limit_bytes=60 * 2**20),
        name="store",
    )(*results)
    shape = keys.shape
    return grad_keys.reshape(shape), grad_values.reshape(shape), grad_gates.reshape(shape), grad_weight


def solution(mesh):
    by_seq = P(("dp", "fsdp"), None, None)
    return jax.shard_map(
        shards,
        mesh=mesh,
        in_specs=(by_seq, P("fsdp", None), by_seq, by_seq, by_seq, by_seq, P()),
        out_specs=(by_seq, by_seq, by_seq, P("fsdp", None)),
        check_vma=False,
    )
```

time: 90.1 us -> 79.9 us (0.89)
  local copies, waits for them, and re-layouts: 9.44 us -> 0 us
    unnamed x18 -> x0, local copies, waits for them, and re-layouts: 9.44 us -> none
    pallas_call x1, Pallas kernels: 79.6 us -> 77 us  [shards(): pl.pallas_call(functools.partial(layer_kernel, lengths.shape[0]), out_sha...]
    pallas_call x0 -> x1, Pallas kernels: none -> 2.08 us  [shards(): pl.pallas_call(store_kernel, out_shape=tuple((jax.ShapeDtypeStruct(r.shap...]
where the time goes in v2:
time: 79.9 us; the launch traced here: 79.7 us
  Pallas kernels  79.1 us (99%)
    pallas_call x1, Pallas kernels, shards(): pl.pallas_call(functools.partial(layer_kernel, lengths.shape[0]), out_sha...  77 us
    pallas_call x1, Pallas kernels, shards(): pl.pallas_call(store_kernel, out_shape=tuple((jax.ShapeDtypeStruct(r.shap...  2.08 us

profile of v2, /device:TPU:1, one launch (start us, length us, event | category | flops | bytes accessed | tf_op | source)
XLA Modules:
  0.0 79.7 jit_solution(13740716797859808201)
XLA Ops:
  0.6 77.0 %layer.1 = (bf16[384,512]{1,0:T(8,128)(2,1)}, bf16[384,512]{1,0:T(8,128)(2,1)}, bf16[384,512]{1,0:T(8,128)(2,1)}, f32[32,512]{1,0:T(8,128)}) custom-call(bf16[384,1024]{1,0:T(8,128)(2,1)} %bitcast.8, bf16[32,512]{1,0:T(8,128)(2,1)} %weight_hbm.1, bf16[384,512]{1,0:T(8,128)(2,1)} %bitcast.9, bf16[384,512]{1,0:T(8,128)(2,1)} %bitcast.10, ...), custom_call_target="tpu_custom_call" | custom-call | tf_op jit(solution)/shard_map/layer/pallas_call | solution.py:388
  77.6 2.1 %store.1 = (bf16[384,512]{1,0:T(8,128)(2,1)}, bf16[384,512]{1,0:T(8,128)(2,1)}, bf16[384,512]{1,0:T(8,128)(2,1)}, f32[32,512]{1,0:T(8,128)}) custom-call(bf16[384,512]{1,0:T(8,128)(2,1)} %get-tuple-element.12.refs_0_, bf16[384,512]{1,0:T(8,128)(2,1)} %get-tuple-element.13.refs_1_, bf16[384,512]{1,0:T(8,128)(2,1)} %get-tuple-element.14.refs_2_, ...), custom_call_target="tpu_custom_call" | custom-call | tf_op jit(solution)/shard_map/store/pallas_call | solution.py:400

commit v3 on v2

--- a/solution.py
+++ b/solution.py
@@ -37,7 +37,7 @@
 def layer_kernel(
     total_seqs,
     events_hbm, weight_hbm, keys_hbm, values_hbm, gates_hbm, upstream_hbm, lengths_hbm,
-    grad_keys_hbm, grad_values_hbm, grad_gates_hbm, grad_weight_ref,
+    grad_keys_hbm, grad_values_hbm, grad_gates_hbm, gw_hbm,
     ev, kk, vv, gg, uu, lens,
     wf, wun, evt, gn, qq, att, dact, gm, gs, gq, out_k, out_v, out_g,
     gbuf, cbuf, sbuf, rbuf, tbuf, zbuf, gw,
@@ -297,14 +297,24 @@
     for store in stores:
         store.start()
 
+    @pl.when(is_source)
+    def _():
+        for send in near_sends:
+            send.wait_send()
+
+    for send in relays + spreads + swaps + core_sends + rs_sends:
+        send.wait_send()
+    for store in stores:
+        store.wait()
+
     head = lax.rem(z // 8 + 4 - x, 4)
+    own_result = pltpu.make_async_copy(gw, gw_hbm.at[core, head], fin_s.at[0])
     final_sends = []
     for dx, dy, swapped in [(dx, dy, k) for dx, dy in OTHER_CHIPS for k in range(2)] + [(0, 0, 1)]:
-        there = gw.at[core, head]
         other_core = 1 - core if swapped else core
         final_sends.append(
             remote(
-                there, there, fin_s.at[dx * 8 + dy * 2 + swapped], fin_r.at[x * 2 + core],
+                gw, gw_hbm.at[core, head], fin_s.at[dx * 8 + dy * 2 + swapped], fin_r.at[x * 2 + core],
                 chip_at(dx, dy, other_core),
             )
         )
@@ -317,49 +327,47 @@
             there = zbuf.at[other]
             remote(there, there, zr_s.at[0], zr_r.at[other], partner).wait_recv()
             acc = acc + zbuf[other].astype(F32)
-        gw[core, head] = (acc * (1.0 / total_seqs)).astype(BF16)
+        gw[...] = (acc * (1.0 / total_seqs)).astype(BF16)
         for send in final_sends:
             send.start()
+        own_result.start()
 
     source_y = lax.rem(z, 4)
     for sx in range(4):
         for sc in range(2):
             @pl.when((chip != sx * 4 + source_y) | (core != sc))
             def _():
-                there = gw.at[sc, lax.rem(z // 8 + 4 - sx, 4)]
-                remote(there, there, fin_s.at[0], fin_r.at[sx * 2 + sc], partner).wait_recv()
-    for half in range(2):
-        for h in range(HEADS):
-            grad_weight_ref[pl.ds(half * 16, 16), pl.ds(h * DEPTH, DEPTH)] = gw[half, h].astype(F32)
-
+                there = gw_hbm.at[sc, lax.rem(z // 8 + 4 - sx, 4)]
+                remote(there, there, fin_s.at[1], fin_r.at[sx * 2 + sc], partner).wait_recv()
     @pl.when(is_source)
     def _():
-        for send in near_sends:
-            send.wait_send()
         for send in final_sends:
             send.wait_send()
-
-    for send in relays + spreads + swaps + core_sends + rs_sends:
-        send.wait_send()
+        own_result.wait()
+
     for target, send in ring_sends:
         @pl.when(target != z)
         def _():
             send.wait_send()
-    for store in stores:
-        store.wait()
 
 
 def store_kernel(*refs):
-    count = (len(refs) - 2) // 3
-    sources, results, held = refs[:count], refs[count : 2 * count], refs[2 * count : 3 * count]
-    in_sem, out_sem = refs[-2:]
+    sources, results, held = refs[:4], refs[4:8], refs[8:12]
+    wide, in_sem, out_sem = refs[12:]
     loads = [pltpu.make_async_copy(a, b, in_sem.at[i]) for i, (a, b) in enumerate(zip(sources, held))]
-    stores = [pltpu.make_async_copy(a, b, out_sem.at[i]) for i, (a, b) in enumerate(zip(held, results))]
+    stores = [
+        pltpu.make_async_copy(a, b, out_sem.at[i]) for i, (a, b) in enumerate(zip((*held[:3], wide), results))
+    ]
     for load in loads:
         load.start()
-    for load, store in zip(loads, stores):
+    for load, store in zip(loads[:3], stores[:3]):
         load.wait()
         store.start()
+    loads[3].wait()
+    for half in range(2):
+        for h in range(HEADS):
+            wide[pl.ds(half * 16, 16), pl.ds(h * DEPTH, DEPTH)] = held[3][half, h].astype(F32)
+    stores[3].start()
     for store in stores:
         store.wait()
 
@@ -380,16 +388,16 @@
         vmem((ROWS, WIDTH), BF16), vmem((ROWS, WIDTH), BF16), vmem((ROWS, WIDTH), BF16),
         vmem((4, 8, 4, 2, 16, 128), BF16), vmem((4, 8, 4, 16, 128), BF16), vmem((4, 8, 4, 16, 128), BF16),
         vmem((16, 4, 2, 16, 128), BF16), vmem((4, 2, 16, 128), BF16), vmem((RING, 16, 128), BF16),
-        vmem((2, 4, 16, 128), BF16),
+        vmem((16, 128), BF16),
         dma((6,)), dma((16,)), dma((4,)), dma((4,)), dma((4,)), dma((64,)), dma((64,)),
         dma((4,)), dma((4,)), dma((4,)), dma((4,)), dma((64,)), dma((64,)), dma((8,)), dma((32,)),
         dma((32,)), dma((8,)), dma((3,)),
     ]
     grad_keys, grad_values, grad_gates, grad_weight = pl.pallas_call(
         functools.partial(layer_kernel, lengths.shape[0]),
-        out_shape=(row_out, row_out, row_out, jax.ShapeDtypeStruct((32, WIDTH), F32)),
+        out_shape=(row_out, row_out, row_out, jax.ShapeDtypeStruct((2, HEADS, 16, DEPTH), BF16)),
         in_specs=[hbm] * 7,
-        out_specs=(hbm, hbm, hbm, pl.BlockSpec(memory_space=vmem)),
+        out_specs=(hbm,) * 4,
         scratch_shapes=scratch,
         compiler_params=pltpu.CompilerParams(
             collective_id=0, has_side_effects=True, vmem_limit_bytes=60 * 2**20
@@ -399,10 +407,10 @@
     results = (grad_keys, grad_values, grad_gates, grad_weight)
     grad_keys, grad_values, grad_gates, grad_weight = pl.pallas_call(
         store_kernel,
-        out_shape=tuple(jax.ShapeDtypeStruct(r.shape, r.dtype) for r in results),
+        out_shape=(row_out, row_out, row_out, jax.ShapeDtypeStruct((32, WIDTH), F32)),
         in_specs=[hbm] * 4,
         out_specs=(hbm,) * 4,
-        scratch_shapes=[vmem(r.shape, r.dtype) for r in results] + [dma((4,)), dma((4,))],
+        scratch_shapes=[vmem(r.shape, r.dtype) for r in results] + [vmem((32, WIDTH), F32), dma((4,)), dma((4,))],
         compiler_params=pltpu.CompilerParams(vmem_limit_bytes=60 * 2**20),
         name="store",
     )(*results)

time: 79.9 us -> 79.2 us (level)
  Pallas kernels: 79.1 us -> 78.3 us
where the time goes in v3:
time: 79.2 us; the launch traced here: 79 us
  Pallas kernels  78.3 us (99%)
    pallas_call x1, Pallas kernels, shards(): pl.pallas_call(functools.partial(layer_kernel, lengths.shape[0]), out_sha...  76.2 us
    pallas_call x1, Pallas kernels, shards(): pl.pallas_call(store_kernel, out_shape=(row_out, row_out, row_out, jax.Sh...  2.08 us

profile of v3, /device:TPU:1, one launch (start us, length us, event | category | flops | bytes accessed | tf_op | source)
XLA Modules:
  0.0 79.0 jit_solution(10542874738890325662)
XLA Ops:
  0.6 76.2 %layer.1 = (bf16[384,512]{1,0:T(8,128)(2,1)}, bf16[384,512]{1,0:T(8,128)(2,1)}, bf16[384,512]{1,0:T(8,128)(2,1)}, bf16[2,4,16,128]{3,2,1,0:T(8,128)(2,1)}) custom-call(bf16[384,1024]{1,0:T(8,128)(2,1)} %bitcast.8, bf16[32,512]{1,0:T(8,128)(2,1)} %weight_hbm.1, bf16[384,512]{1,0:T(8,128)(2,1)} %bitcast.9, bf16[384,512]{1,0:T(8,128)(2,1)} %bitcast.10, ...), custom_call_target="tpu_custom_call" | custom-call | tf_op jit(solution)/shard_map/layer/pallas_call | solution.py:396
  76.9 2.1 %store.1 = (bf16[384,512]{1,0:T(8,128)(2,1)}, bf16[384,512]{1,0:T(8,128)(2,1)}, bf16[384,512]{1,0:T(8,128)(2,1)}, f32[32,512]{1,0:T(8,128)}) custom-call(bf16[384,512]{1,0:T(8,128)(2,1)} %get-tuple-element.12.refs_0_, bf16[384,512]{1,0:T(8,128)(2,1)} %get-tuple-element.13.refs_1_, bf16[384,512]{1,0:T(8,128)(2,1)} %get-tuple-element.14.refs_2_, ...), custom_call_target="tpu_custom_call" | custom-call | tf_op jit(solution)/shard_map/store/pallas_call | solution.py:408
